TPU v7x, 32 devices: a whole 2x2x4 slice. The times are simulated.
32 devices in a mesh: spec: 8 (over y, x, core), wave: 4 (over z).
Axes of the slice: x: 2, y: 2, z: 4, core: 2. Of those that a mesh axis runs over, the one named last changes fastest.
Arguments:
- spectra: bfloat16 [8192, 7168], P('spec', 'wave'), may hold values from 0.049804688 to 5
- offsets: int32 [32], P('spec'), may hold values from 0 to 7167, as said below
- cover_lo: int32 [8192], P('spec'), may hold values from 0 to 7167, as said below
- cover_hi: int32 [8192], P('spec'), may hold values from 5377 to 7168
- coefficients: float32 [8192, 128], P('spec'), may hold values from 0.03 to 0.3
- templates: float32 [128, 7168], P(None, 'wave'), may hold values from 0.03 to 0.3
Outputs:
- templates_new: float32 [128, 7168], P(None, 'wave')
- coefficients_new: float32 [8192, 128], P('spec')
Inputs may be any that keep to these rules, and one draw needn't show every extreme that they name: `offsets`: the first block of each index of spec has an offset of at least 5376; the last block's offset is 7167. cover_lo < cover_hi for every spectrum; about one spectrum in eight has weight one only on its last 1 to 4 observed pixels, cover_hi = 7168; the others have cover_lo < 1792 and cover_hi > 5376.
All inputs are finite; a program needn't handle non-finite values.
Results may differ from a plain program's by a relative error of at most 0.0012.
Values may be sent and summed in bfloat16 or wider, within the bound.
A program may use at most 128 MiB of HBM per device.

v0:
```python
import jax
import jax.numpy as jnp
from jax import lax
from jax.sharding import PartitionSpec as P

ITERS = 4


def take_blocks(joined, starts, blocks, width):
    rows = joined.shape[0]
    grouped = joined.reshape(blocks, rows // blocks, joined.shape[1])
    picked = jax.vmap(lambda piece, start: lax.dynamic_slice_in_dim(piece, start, width, 1))(
        grouped, starts
    )
    return picked.reshape(rows, width)


def ratio_of(rest, weight, coef_bf, temps_bf):
    model = jnp.dot(coef_bf, temps_bf, preferred_element_type=jnp.float32)
    inside = weight > 0
    return jnp.where(inside, rest.astype(jnp.float32) / jnp.where(inside, model, 1.0), 0.0).astype(
        jnp.bfloat16
    )


def over_rows(left, right):
    return lax.dot_general(
        left, right, (((0,), (0,)), ((), ())), preferred_element_type=jnp.float32
    )


def over_pixels(left, right):
    return lax.dot_general(
        left, right, (((1,), (1,)), ((), ())), preferred_element_type=jnp.float32
    )


def template_update(temps, num_t, den_t):
    num_a, den_a = lax.psum((num_t, den_t), "spec")
    return temps * num_a / jnp.maximum(den_a, 1.0)


def coef_update(coef, num_c, den_c):
    num_a, den_a = lax.psum((num_c, den_c), "wave")
    return coef * num_a / jnp.maximum(den_a, 1.0)


def shards(spectra, offsets, cover_lo, cover_hi, coefficients, templates):
    rows, width = spectra.shape
    blocks = offsets.shape[0]
    block_rows = rows // blocks
    wave_pos = lax.axis_index("wave")
    row_off = jnp.repeat(offsets, block_rows)
    whole = lax.all_gather(spectra, "wave", axis=1, tiled=True)
    joined = jnp.concatenate([whole, jnp.zeros((rows, width), whole.dtype)], axis=1)
    starts = jnp.minimum(wave_pos * width + offsets, whole.shape[1])
    rest = take_blocks(joined, starts, blocks, width)
    pixel = wave_pos * width + jnp.arange(width, dtype=jnp.int32)
    observed = pixel[None, :] + row_off[:, None]
    weight = ((observed >= cover_lo[:, None]) & (observed < cover_hi[:, None])).astype(jnp.bfloat16)
    temps = templates
    coef = coefficients
    for update in range(ITERS):
        coef_bf = coef.astype(jnp.bfloat16)
        ratio = ratio_of(rest, weight, coef_bf, temps.astype(jnp.bfloat16))
        temps = template_update(temps, over_rows(coef_bf, ratio), over_rows(coef_bf, weight))
        temps_bf = temps.astype(jnp.bfloat16)
        ratio_new = ratio_of(rest, weight, coef_bf, temps_bf)
        coef = coef_update(coef, over_pixels(ratio_new, temps_bf), over_pixels(weight, temps_bf))
    return (temps, coef)


def solution(mesh):
    in_specs = (
        P("spec", "wave"),
        P("spec"),
        P("spec"),
        P("spec"),
        P("spec", None),
        P(None, "wave"),
    )
    out_specs = (P(None, "wave"), P("spec", None))
    return jax.shard_map(shards, mesh=mesh, in_specs=in_specs, out_specs=out_specs, check_vma=False)
```

profile of v0, /device:TPU:24, one launch (start us, length us, event | category | flops | bytes accessed | tf_op | source)
XLA Modules:
  0.0 828.9 jit_solution(14119728213163925143)
XLA Ops:
  7.2 0.0 all-gather.2.cloned.1.call-start
  7.2 0.7 all-gather.2.cloned.1.call-update
  7.9 0.0 all-reduce.25.cloned.1.call-start
  8.0 0.7 broadcast_bitcast_fusion
  8.7 0.7 fusion.30
  9.4 0.1 copy.8
  9.5 4.5 convolution_bitcast_fusion.1
  14.0 246.0 %all-gather.2.cloned.1.call-done = bf16[1024,7168]{1,0:T(8,128)(2,1)} async-done(((bf16[1024,1792]{1,0:T(8,128)(2,1)}), bf16[1024,7168]{1,0:T(8,128)(2,1)}) %all-gather.2.cloned.1.call-update) | async-done | bytes 14680080 | tf_op jit(solution)/shard_map/all_gather | solution.py:54
  260.0 13.1 %concatenate.6 = bf16[1024,8960]{1,0:T(8,128)(2,1)} pad(bf16[1024,7168]{1,0:T(8,128)(2,1)} %all-gather.2.cloned.1.call-done, bf16[]{:T(256)} %constant.10.clone.1), padding=0_0x0_1792 | pad | bytes 33030146 | tf_op jit(solution)/shard_map/concatenate | solution.py:55
  273.2 17.9 %while.1 = (s32[]{:T(128)}, bf16[4,256,8960]{2,1,0:T(8,128)(2,1)}, s32[4,3]{1,0:T(4,128)S(1)}, bf16[4,256,1792]{2,1,0:T(8,128)(2,1)}, s32[]{:T(128)}) while((s32[]{:T(128)}, bf16[4,256,8960]{2,1,0:T(8,128)(2,1)}, s32[4,3]{1,0:T(4,128)S(1)}, bf16[4,256,1792]{2,1,0:T(8,128)(2,1)}, s32[]{:T(128)}) %tuple.54), condition=%wide.while_cond, body=%wide.while_body.sunk | while | flops 2 | bytes 1836649 | solution.py:12
  273.2 0.6 fusion.106
  273.8 3.8 dynamic-slice_dynamic-update-slice_fusion.2
  277.6 0.7 fusion.106
  278.3 3.8 dynamic-slice_dynamic-update-slice_fusion.2
  282.1 0.7 fusion.106
  282.8 3.8 dynamic-slice_dynamic-update-slice_fusion.2
  286.6 0.7 fusion.106
  287.3 3.8 dynamic-slice_dynamic-update-slice_fusion.2
  291.1 6.5 convolution_bitcast_fusion
  297.6 0.0 all-reduce.25.cloned.1.call-update
  297.6 0.0 all-reduce.33.cloned.1.call-start
  297.7 0.3 copy.9
  298.0 61.5 %all-reduce.25.cloned.1.call-done = (f32[128,1792]{0,1:T(8,128)}, f32[128,1792]{0,1:T(8,128)}) async-done(((f32[128,1792]{0,1:T(8,128)}, f32[128,1792]{0,1:T(8,128)}), (f32[128,1792]{0,1:T(8,128)}, f32[128,1792]{0,1:T(8,128)})) %all-reduce.25.cloned.1.call-update) | async-done | bytes 1835024 | tf_op jit(solution)/shard_map/psum | solution.py:39
  359.4 1.6 maximum_divide_fusion.3
  361.0 5.8 fusion.23
  366.8 2.8 fusion.61
  369.6 0.0 all-reduce.33.cloned.1.call-update
  369.7 0.2 all-reduce.23.cloned.1.call-start
  369.9 49.7 %all-reduce.33.cloned.1.call-done = (f32[1024,128]{1,0:T(8,128)}, f32[1024,128]{1,0:T(8,128)}) async-done(((f32[1024,128]{1,0:T(8,128)}, f32[1024,128]{1,0:T(8,128)}), (f32[1024,128]{1,0:T(8,128)}, f32[1024,128]{1,0:T(8,128)})) %all-reduce.33.cloned.1.call-update) | async-done | bytes 1048592 | tf_op jit(solution)/shard_map/psum | solution.py:44
  419.6 1.3 maximum_divide_fusion.7
  420.8 7.1 fusion.19
  427.9 3.5 fusion.55
  431.4 0.0 all-reduce.23.cloned.1.call-update
  431.4 0.0 all-reduce.31.cloned.1.call-start
  431.5 61.4 %all-reduce.23.cloned.1.call-done = (f32[128,1792]{0,1:T(8,128)}, f32[128,1792]{0,1:T(8,128)}) async-done(((f32[128,1792]{0,1:T(8,128)}, f32[128,1792]{0,1:T(8,128)}), (f32[128,1792]{0,1:T(8,128)}, f32[128,1792]{0,1:T(8,128)})) %all-reduce.23.cloned.1.call-update) | async-done | bytes 1835024 | tf_op jit(solution)/shard_map/psum | solution.py:39
  492.8 1.6 maximum_divide_fusion.2
  494.4 5.8 fusion.22
  500.3 2.8 fusion.49
  503.1 0.0 all-reduce.31.cloned.1.call-update
  503.1 0.3 all-reduce.21.cloned.1.call-start
  503.3 49.6 %all-reduce.31.cloned.1.call-done = (f32[1024,128]{1,0:T(8,128)}, f32[1024,128]{1,0:T(8,128)}) async-done(((f32[1024,128]{1,0:T(8,128)}, f32[1024,128]{1,0:T(8,128)}), (f32[1024,128]{1,0:T(8,128)}, f32[1024,128]{1,0:T(8,128)})) %all-reduce.31.cloned.1.call-update) | async-done | bytes 1048592 | tf_op jit(solution)/shard_map/psum | solution.py:44
  553.0 1.3 maximum_divide_fusion.6
  554.3 7.1 fusion.18
  561.3 3.5 fusion.43
  564.8 0.0 all-reduce.21.cloned.1.call-update
  564.8 0.0 all-reduce.29.cloned.1.call-start
  564.9 61.4 %all-reduce.21.cloned.1.call-done = (f32[128,1792]{0,1:T(8,128)}, f32[128,1792]{0,1:T(8,128)}) async-done(((f32[128,1792]{0,1:T(8,128)}, f32[128,1792]{0,1:T(8,128)}), (f32[128,1792]{0,1:T(8,128)}, f32[128,1792]{0,1:T(8,128)})) %all-reduce.21.cloned.1.call-update) | async-done | bytes 1835024 | tf_op jit(solution)/shard_map/psum | solution.py:39
  626.3 1.6 maximum_divide_fusion.1
  627.8 5.8 fusion.21
  633.7 2.8 fusion.37
  636.5 0.0 all-reduce.29.cloned.1.call-update
  636.5 0.3 all-reduce.19.cloned.1.call-start
  636.8 49.6 %all-reduce.29.cloned.1.call-done = (f32[1024,128]{1,0:T(8,128)}, f32[1024,128]{1,0:T(8,128)}) async-done(((f32[1024,128]{1,0:T(8,128)}, f32[1024,128]{1,0:T(8,128)}), (f32[1024,128]{1,0:T(8,128)}, f32[1024,128]{1,0:T(8,128)})) %all-reduce.29.cloned.1.call-update) | async-done | bytes 1048592 | tf_op jit(solution)/shard_map/psum | solution.py:44
  686.4 1.3 maximum_divide_fusion.5
  687.7 7.1 fusion.17
  694.8 3.5 fusion.31
  698.2 0.0 all-reduce.27.cloned.1.call-start
  698.3 61.4 %all-reduce.19.cloned.1.call-done = (f32[128,1792]{0,1:T(8,128)}, f32[128,1792]{0,1:T(8,128)}) async-done(((f32[128,1792]{0,1:T(8,128)}, f32[128,1792]{0,1:T(8,128)}), (f32[128,1792]{0,1:T(8,128)}, f32[128,1792]{0,1:T(8,128)})) %all-reduce.19.cloned.1.call-update) | async-done | bytes 1835024 | tf_op jit(solution)/shard_map/psum | solution.py:39
  759.7 1.6 maximum_divide_fusion
  761.3 5.8 fusion.20
  767.1 2.8 fusion.28
  769.9 1.2 copy.16
  771.1 48.7 %all-reduce.27.cloned.1.call-done = (f32[1024,128]{1,0:T(8,128)}, f32[1024,128]{1,0:T(8,128)}) async-done(((f32[1024,128]{1,0:T(8,128)}, f32[1024,128]{1,0:T(8,128)}), (f32[1024,128]{1,0:T(8,128)}, f32[1024,128]{1,0:T(8,128)})) %all-reduce.27.cloned.1.call-update) | async-done | bytes 1048592 | tf_op jit(solution)/shard_map/psum | solution.py:44
  819.8 2.1 maximum_divide_fusion.4
  (19 shorter events, 0.1 us)
Async XLA Ops:
  7.2 252.8 %all-gather.2.cloned.1.call-start = ((), (), s32[]{:S(2)}) async-start(), calls=%async_computation | async-start | bytes 18350080 | tf_op jit(solution)/shard_map/all_gather | solution.py:54
  7.9 351.5 %all-reduce.25.cloned.1.call-start = ((), (), s32[]{:S(2)}) async-start(), calls=%async_computation.4 | async-start | bytes 3670016 | tf_op jit(solution)/shard_map/psum | solution.py:39
  273.1 17.9 %copy-start = (f32[128,1792]{1,0:T(8,128)S(1)}, f32[128,1792]{1,0:T(8,128)}, u32[]{:S(2)}) copy-start(f32[128,1792]{1,0:T(8,128)} %param.11) | copy-start | bytes 2752516
  273.1 17.9 %copy-start.1 = (f32[1024,128]{1,0:T(8,128)S(1)}, f32[1024,128]{1,0:T(8,128)}, u32[]{:S(2)}) copy-start(f32[1024,128]{1,0:T(8,128)} %param.10) | copy-start | bytes 1572868
  273.1 17.9 %copy-start.2 = (s32[1024]{0:T(1024)S(1)}, s32[1024]{0:T(1024)}, u32[]{:S(2)}) copy-start(s32[1024]{0:T(1024)} %param.9) | copy-start | bytes 12292
  273.1 17.9 %copy-start.3 = (s32[1024]{0:T(1024)S(1)}, s32[1024]{0:T(1024)}, u32[]{:S(2)}) copy-start(s32[1024]{0:T(1024)} %param.8) | copy-start | bytes 12292
  297.6 122.0 %all-reduce.33.cloned.1.call-start = ((), (), s32[]{:S(2)}) async-start(), calls=%async_computation.8 | async-start | bytes 2097152 | tf_op jit(solution)/shard_map/psum | solution.py:44
  369.7 123.2 %all-reduce.23.cloned.1.call-start = ((), (), s32[]{:S(2)}) async-start(), calls=%async_computation.3 | async-start | bytes 3670016 | tf_op jit(solution)/shard_map/psum | solution.py:39
  431.4 121.6 %all-reduce.31.cloned.1.call-start = ((), (), s32[]{:S(2)}) async-start(), calls=%async_computation.7 | async-start | bytes 2097152 | tf_op jit(solution)/shard_map/psum | solution.py:44
  503.1 123.2 %all-reduce.21.cloned.1.call-start = ((), (), s32[]{:S(2)}) async-start(), calls=%async_computation.2 | async-start | bytes 3670016 | tf_op jit(solution)/shard_map/psum | solution.py:39
  564.8 121.6 %all-reduce.29.cloned.1.call-start = ((), (), s32[]{:S(2)}) async-start(), calls=%async_computation.6 | async-start | bytes 2097152 | tf_op jit(solution)/shard_map/psum | solution.py:44
  636.5 123.2 %all-reduce.19.cloned.1.call-start = ((), (), s32[]{:S(2)}) async-start(), calls=%async_computation.1 | async-start | bytes 3670016 | tf_op jit(solution)/shard_map/psum | solution.py:39
  698.2 121.6 %all-reduce.27.cloned.1.call-start = ((), (), s32[]{:S(2)}) async-start(), calls=%async_computation.5 | async-start | bytes 2097152 | tf_op jit(solution)/shard_map/psum | solution.py:44
Sparse Core Ops, SparseCore 0:
  9.6 250.3 all-gather.1
  297.7 61.6 all-reduce.24
  369.8 49.7 all-reduce.32
  431.5 61.2 all-reduce.22
  503.2 49.7 all-reduce.30
  565.0 61.2 all-reduce.20
  636.6 49.7 all-reduce.28
  698.4 61.2 all-reduce.18
  770.0 49.7 all-reduce.26
where the time goes:
time: 841 us; the launch traced here: 829 us
  waiting for transfers between devices  690 us (82%)
  matrix products  77.2 us (9%)
  local copies, waits for them, and re-layouts  33.4 us (4%)
  between operations  14.4 us (2%)
  other arithmetic  12.9 us (2%)
    all_gather x1, waiting for transfers between devices, shards(): whole = lax.all_gather(spectra, 'wave', axis=1, tiled=True)  246 us
    psum x4, waiting for transfers between devices, template_update(): num_a, den_a = lax.psum((num_t, den_t), 'spec')  246 us
    psum x4, waiting for transfers between devices, coef_update(): num_a, den_a = lax.psum((num_c, den_c), 'wave')  198 us
    dot_general x8, matrix products, over_rows(): lax.dot_general(left, right, (((0,), (0,)), ((), ())), preferred_element_...  42.7 us
    dot_general x8, matrix products, over_pixels(): lax.dot_general(left, right, (((1,), (1,)), ((), ())), preferred_element_...  34.5 us
    gather x12, local copies, waits for them, and re-layouts  17.9 us
  transfers between devices with their start and end apart: 9, of which 9 were waited for; matrix products, arithmetic and copies ran while one was open for 1% of the time, Pallas kernels for 0%

commit v1 on v0

v1 whole, which is shorter than its diff:
```python
import functools

import jax
import jax.numpy as jnp
from jax import lax
from jax.experimental import pallas as pl
from jax.experimental.pallas import tpu as pltpu
from jax.sharding import PartitionSpec as P

ITERS = 4
LANES = 128
MESH = pl.DeviceIdType.MESH
F32 = jnp.float32
BF16 = jnp.bfloat16


def shift_kernel(shift_ref, flux_ref, lo_ref, hi_ref, out_ref):
    shift = shift_ref[pl.program_id(0)]
    rows, width = flux_ref.shape
    lane = lax.broadcasted_iota(jnp.int32, (rows, LANES), 1)
    before = jnp.zeros((rows, LANES), F32)
    for tile in range(width // LANES + 1):
        if tile < width // LANES:
            now = flux_ref[:, tile * LANES : (tile + 1) * LANES].astype(F32)
            now = pltpu.roll(now, shift, 1)
        else:
            now = jnp.zeros((rows, LANES), F32)
        moved = jnp.where(lane < shift, before, now)
        column = lane + tile * LANES
        inside = (column >= lo_ref[...]) & (column < hi_ref[...])
        out_ref[:, tile * LANES : (tile + 1) * LANES] = jnp.where(inside, moved, 0.0).astype(BF16)
        before = now


def shifted_rest(spectra, shift, low, high, blocks):
    rows, width = spectra.shape
    per = rows // blocks
    return pl.pallas_call(
        shift_kernel,
        out_shape=jax.ShapeDtypeStruct((rows, width + LANES), BF16),
        grid_spec=pltpu.PrefetchScalarGridSpec(
            num_scalar_prefetch=1,
            grid=(blocks,),
            in_specs=[
                pl.BlockSpec((per, width), lambda i, s: (i, 0)),
                pl.BlockSpec((per, LANES), lambda i, s: (i, 0)),
                pl.BlockSpec((per, LANES), lambda i, s: (i, 0)),
            ],
            out_specs=pl.BlockSpec((per, width + LANES), lambda i, s: (i, 0)),
        ),
        compiler_params=pltpu.CompilerParams(vmem_limit_bytes=32 * 2**20),
    )(shift, spectra, low, high)


def main_kernel(
    n_spec,
    n_wave,
    first_ref,
    rest_ref,
    lo_ref,
    hi_ref,
    coef_ref,
    temp_ref,
    temps_out,
    coef_out,
    wbuf,
    wown,
    wfin,
    hb,
    hown,
    hfin,
    parts,
    send_a,
    recv_a,
    send_b,
    recv_b,
    send_z,
    recv_z,
    stat_c,
    recv_c,
    s_a,
    r_a,
    s_b,
    r_b,
    s_z,
    r_z,
    s_w,
    r_w,
    s_wb,
    r_wb,
    s_wc,
    r_wc,
    s_c,
    r_c,
    s_h,
    r_h,
    s_f,
    r_f,
    s_g,
    r_g,
):
    spec = lax.axis_index("spec")
    wave = lax.axis_index("wave")
    chips = n_spec // 2
    chip = spec // 2
    core = spec % 2
    buddy = 1 - core
    rows, _ = hb.shape
    blocks = first_ref.shape[0]
    per = rows // blocks
    own = rows // n_wave
    tiles = wbuf.shape[1]
    chunk = tiles // n_wave
    rank_part = wbuf.shape[2]
    rank = n_spec * rank_part
    spans = rest_ref.shape[1] // LANES
    group = max(g for g in range(1, 6) if spans % g == 0)
    own_rows = pl.ds(pl.multiple_of(wave * own, own), own)

    def to_chip(k):
        return (lax.rem(chip + k, chips) * 2 + core, wave)

    def to_buddy():
        return (chip * 2 + buddy, wave)

    def to_wave(k):
        return (spec, lax.rem(wave + k, n_wave))

    def to_spec(k):
        return (lax.rem(spec + k, n_spec), wave)

    def copy(src, dst, send, recv, device):
        return pltpu.make_async_remote_copy(
            src_ref=src, dst_ref=dst, send_sem=send, recv_sem=recv, device_id=device, device_id_type=MESH
        )

    def part_of(k):
        return pl.ds(lax.rem(wave + k, n_wave) * chunk, chunk)

    def part_from(k):
        return pl.ds(lax.rem(wave + n_wave - k, n_wave) * chunk, chunk)

    barrier = pltpu.get_barrier_semaphore()
    for k in range(1, n_spec):
        pl.semaphore_signal(barrier, inc=1, device_id=to_spec(k), device_id_type=MESH)
    for k in range(1, n_wave):
        pl.semaphore_signal(barrier, inc=1, device_id=to_wave(k), device_id_type=MESH)
    pl.semaphore_wait(barrier, n_spec + n_wave - 2)

    def gather_templates():
        over_z = [None] + [
            copy(wbuf.at[spec, part_of(0)], wbuf.at[spec, part_of(0)], s_w.at[k], r_w.at[k], to_wave(k))
            for k in range(1, n_wave)
        ]
        over_chips = {}
        over_core = {}
        for kz in range(n_wave):
            for k in range(chips):
                slot = wbuf.at[lax.rem(chip + chips - k, chips) * 2 + core, part_from(kz)]
                over_core[kz, k] = copy(slot, slot, s_wc.at[kz, k], r_wc.at[kz, k], to_buddy())
                if k:
                    mine = wbuf.at[spec, part_from(kz)]
                    over_chips[kz, k] = copy(mine, mine, s_wb.at[kz, k], r_wb.at[kz, k], to_chip(k))
        for k in range(1, n_wave):
            over_z[k].start()
        for kz in range(n_wave):
            if kz:
                over_z[kz].wait_recv()
            for k in range(1, chips):
                over_chips[kz, k].start()
            over_core[kz, 0].start()
        for kz in range(n_wave):
            for k in range(1, chips):
                over_chips[kz, k].wait_recv()
                over_core[kz, k].start()
        for kz in range(n_wave):
            for k in range(chips):
                over_core[kz, k].wait()
                if k:
                    over_chips[kz, k].wait_send()
            if kz:
                over_z[kz].wait_send()

    def tile_of(index):
        piece = wbuf[:, index]
        if rank_part % 16:
            return piece.astype(F32).reshape(rank, LANES).astype(BF16)
        return piece.reshape(rank, LANES)

    def ratio_of(block, g):
        at = pl.ds(pl.multiple_of(block * per, per), per)
        start = first_ref[block] + g * group
        temps = jnp.concatenate(
            [tile_of(jnp.clip(start + k, 0, tiles - 1)) for k in range(group)], axis=1
        )
        model = jnp.dot(hb[at, :], temps, preferred_element_type=F32)
        rest = rest_ref[at, g * group * LANES : (g + 1) * group * LANES].astype(F32)
        return temps, jnp.where(rest > 0, rest / model, 0.0).astype(BF16)

    def put_stat(index, value):
        for part in range(n_spec):
            send_a[part % 2, part // 2, index] = value[part * rank_part : (part + 1) * rank_part]

    def mask_of(low, high, first):
        pixel = lax.broadcasted_iota(jnp.int32, low.shape, 1) + first
        return jnp.where((pixel >= low) & (pixel < high), 1.0, 0.0).astype(BF16)

    wown[...] = temp_ref[...]
    wbuf[spec, part_of(0)] = temp_ref[...].astype(BF16)
    hb[...] = coef_ref[...].astype(BF16)
    hown[...] = coef_ref[own_rows, :]
    for block in range(blocks):
        parts[block, 0] = jnp.zeros((rank, LANES), F32)
        parts[block, spans + 1] = jnp.zeros((rank, LANES), F32)
    gather_templates()

    last_temps = [
        copy(wown, wfin.at[spec], s_f.at[k], r_f.at[k], to_spec(k)) for k in range(1, n_spec)
    ]
    order = list(range(1, n_wave)) + [0]

    def update(step, unused):
        def block_stats(block, unused):
            at = pl.ds(pl.multiple_of(block * per, per), per)
            for g in range(spans // group):
                temps, ratio = ratio_of(block, g)
                num = lax.dot_general(
                    hb[at, :], ratio, (((0,), (0,)), ((), ())), preferred_element_type=F32
                )
                for k in range(group):
                    parts[block, 1 + g * group + k] = num[:, k * LANES : (k + 1) * LANES]
            return 0

        lax.fori_loop(0, blocks, block_stats, 0)

        copies_a = {}
        copies_b = {}
        for kz in range(n_wave + 1):
            where = part_of(kz) if kz < n_wave else pl.ds(tiles, chunk)
            copies_a[kz] = copy(
                send_a.at[buddy, :, where], recv_a.at[:, where], s_a.at[kz], r_a.at[kz], to_buddy()
            )
            for k in range(1, chips):
                copies_b[kz, k] = copy(
                    send_b.at[lax.rem(chip + k, chips), where],
                    recv_b.at[k - 1, where],
                    s_b.at[kz, k],
                    r_b.at[kz, k],
                    to_chip(k),
                )
        copies_z = {
            k: copy(send_z.at[part_of(k)], recv_z.at[k - 1], s_z.at[k], r_z.at[k], to_wave(k))
            for k in range(1, n_wave)
        }

        for kz in order:
            first = lax.rem(wave + kz, n_wave) * chunk

            def add_blocks(i, unused):
                index = first + i
                total = parts[0, jnp.clip(index - first_ref[0], -1, spans) + 1]
                for block in range(1, blocks):
                    total = total + parts[block, jnp.clip(index - first_ref[block], -1, spans) + 1]
                put_stat(index, total)
                return 0

            lax.fori_loop(0, chunk, add_blocks, 0)
            copies_a[kz].start()

        def den_tile(i, unused):
            mask = mask_of(lo_ref[...], hi_ref[...], (wave * chunk + i) * LANES)
            put_stat(
                tiles + i,
                lax.dot_general(hb[...], mask, (((0,), (0,)), ((), ())), preferred_element_type=F32),
            )
            return 0

        lax.fori_loop(0, chunk, den_tile, 0)
        copies_a[n_wave].start()

        for kz in order + [n_wave]:
            first = lax.rem(wave + kz, n_wave) * chunk if kz < n_wave else tiles
            copies_a[kz].wait_recv()

            def add_core(i, unused):
                for c in range(chips):
                    send_b[c, first + i] = (
                        send_a[core, c, first + i] + recv_a[c, first + i]
                    ).astype(send_b.dtype)
                return 0

            lax.fori_loop(0, chunk, add_core, 0)
            for k in range(1, chips):
                copies_b[kz, k].start()

        def chip_sum(index):
            total = send_a[core, chip, index] + recv_a[chip, index]
            for k in range(1, chips):
                total = total + recv_b[k - 1, index].astype(F32)
            return total

        for kz in order[:-1]:
            first = lax.rem(wave + kz, n_wave) * chunk
            for k in range(1, chips):
                copies_b[kz, k].wait_recv()

            def add_chips(i, unused):
                send_z[first + i] = chip_sum(first + i)
                return 0

            lax.fori_loop(0, chunk, add_chips, 0)
            copies_z[kz].start()
        for kz in (0, n_wave):
            for k in range(1, chips):
                copies_b[kz, k].wait_recv()
        for k in range(1, n_wave):
            copies_z[k].wait_recv()

        def new_tile(i, unused):
            num = chip_sum(wave * chunk + i)
            for k in range(1, n_wave):
                num = num + recv_z[k - 1, i]
            value = wown[i] * num / jnp.maximum(chip_sum(tiles + i), 1.0)
            wown[i] = value
            wbuf[spec, wave * chunk + i] = value.astype(BF16)
            return 0

        lax.fori_loop(0, chunk, new_tile, 0)
        for kz in range(n_wave + 1):
            copies_a[kz].wait_send()
            for k in range(1, chips):
                copies_b[kz, k].wait_send()
        for k in range(1, n_wave):
            copies_z[k].wait_send()

        gather_templates()

        @pl.when(step == ITERS - 1)
        def _():
            for one in last_temps:
                one.start()

        def block_coefs(block, unused):
            at = pl.ds(pl.multiple_of(block * per, per), per)
            total = jnp.zeros((per, rank), F32)
            for g in range(spans // group):
                temps, ratio = ratio_of(block, g)
                total = total + lax.dot_general(
                    ratio, temps, (((1,), (1,)), ((), ())), preferred_element_type=F32
                )
            stat_c[at, :] = total
            return 0

        lax.fori_loop(0, blocks, block_coefs, 0)
        copies_c = []
        for k in range(1, n_wave):
            theirs = pl.ds(pl.multiple_of(lax.rem(wave + k, n_wave) * own, own), own)
            copies_c.append(
                copy(stat_c.at[theirs], recv_c.at[k - 1], s_c.at[k], r_c.at[k], to_wave(k))
            )
        for one in copies_c:
            one.start()

        def den_coef(i, total):
            masks = []
            temps = []
            for k in range(4):
                masks.append(mask_of(lo_ref[own_rows, :], hi_ref[own_rows, :], (i * 4 + k) * LANES))
                temps.append(tile_of(i * 4 + k))
            return total + lax.dot_general(
                jnp.concatenate(masks, axis=1),
                jnp.concatenate(temps, axis=1),
                (((1,), (1,)), ((), ())),
                preferred_element_type=F32,
            )

        den = lax.fori_loop(0, tiles // 4, den_coef, jnp.zeros((own, rank), F32))
        for one in copies_c:
            one.wait_recv()
        num = stat_c[own_rows, :]
        for k in range(1, n_wave):
            num = num + recv_c[k - 1]
        value = hown[...] * num / jnp.maximum(den, 1.0)
        hown[...] = value
        for one in copies_c:
            one.wait_send()

        @pl.when(step < ITERS - 1)
        def _():
            hb[own_rows, :] = value.astype(BF16)
            copies_h = [
                copy(hb.at[own_rows], hb.at[own_rows], s_h.at[k], r_h.at[k], to_wave(k))
                for k in range(1, n_wave)
            ]
            for one in copies_h:
                one.start()
            for one in copies_h:
                one.wait()

        return 0

    lax.fori_loop(0, ITERS, update, 0)

    last_coefs = [
        copy(hown, hfin.at[wave], s_g.at[k], r_g.at[k], to_wave(k)) for k in range(1, n_wave)
    ]
    for one in last_coefs:
        one.start()
    wfin[spec] = wown[...]
    hfin[wave] = hown[...]
    for one in last_temps:
        one.wait()
    for i in range(chunk):
        temps_out[:, i * LANES : (i + 1) * LANES] = wfin[:, i].reshape(rank, LANES)
    for one in last_coefs:
        one.wait()
    for k in range(n_wave):
        coef_out[k * own : (k + 1) * own, :] = hfin[k]


def shards(n_spec, n_wave, spectra, offsets, cover_lo, cover_hi, coefficients, templates):
    rows, width = spectra.shape
    rank = templates.shape[0]
    blocks = offsets.shape[0]
    chips = n_spec // 2
    chunk = width // LANES
    tiles = chunk * n_wave
    part = rank // n_spec
    own = rows // n_wave
    wave = lax.axis_index("wave")
    spec = lax.axis_index("spec")

    base = wave * width - offsets
    shift = jnp.mod(base, LANES)
    first = (base - shift) // LANES
    row_off, row_shift = (jnp.repeat(v, rows // blocks) for v in (offsets, shift))
    begin = wave * width
    low = jnp.maximum(jnp.maximum(cover_lo - begin, 0), row_off - begin) + row_shift
    high = jnp.minimum(cover_hi - begin, width) + row_shift

    def spread(value):
        return jnp.broadcast_to(value[:, None], (rows, LANES))

    rest = shifted_rest(spectra, shift, spread(low), spread(high), blocks)
    mine = lax.dynamic_slice_in_dim(templates, spec * part, part, 0)
    mine = mine.reshape(part, chunk, LANES).transpose(1, 0, 2)

    vmem = pl.BlockSpec(memory_space=pltpu.VMEM)
    dma = pltpu.SemaphoreType.DMA
    return pl.pallas_call(
        functools.partial(main_kernel, n_spec, n_wave),
        out_shape=(
            jax.ShapeDtypeStruct((rank, width), F32),
            jax.ShapeDtypeStruct((rows, rank), F32),
        ),
        in_specs=[pl.BlockSpec(memory_space=pltpu.SMEM)] + [vmem] * 5,
        out_specs=(vmem, vmem),
        scratch_shapes=[
            pltpu.VMEM((n_spec, tiles, part, LANES), BF16),
            pltpu.VMEM((chunk, part, LANES), F32),
            pltpu.VMEM((n_spec, chunk, part, LANES), F32),
            pltpu.VMEM((rows, rank), BF16),
            pltpu.VMEM((own, rank), F32),
            pltpu.VMEM((n_wave, own, rank), F32),
            pltpu.VMEM((blocks, chunk + 3, rank, LANES), F32),
            pltpu.VMEM((2, chips, tiles + chunk, part, LANES), F32),
            pltpu.VMEM((chips, tiles + chunk, part, LANES), F32),
            pltpu.VMEM((chips, tiles + chunk, part, LANES), F32),
            pltpu.VMEM((chips - 1, tiles + chunk, part, LANES), F32),
            pltpu.VMEM((tiles, part, LANES), F32),
            pltpu.VMEM((n_wave - 1, chunk, part, LANES), F32),
            pltpu.VMEM((rows, rank), F32),
            pltpu.VMEM((n_wave - 1, own, rank), F32),
        ]
        + [dma((n_wave + 1,))] * 2
        + [dma((n_wave + 1, chips))] * 2
        + [dma((n_wave,))] * 2
        + [dma((n_wave,))] * 2
        + [dma((n_wave, chips))] * 4
        + [dma((n_wave,))] * 2
        + [dma((n_wave,))] * 2
        + [dma((n_spec,))] * 2
        + [dma((n_wave,))] * 2,
        compiler_params=pltpu.CompilerParams(
            collective_id=0, has_side_effects=True, vmem_limit_bytes=48 * 2**20
        ),
    )(
        first,
        rest,
        spread(cover_lo - row_off),
        spread(cover_hi - row_off),
        coefficients,
        mine,
    )


def solution(mesh):
    in_specs = (
        P("spec", "wave"),
        P("spec"),
        P("spec"),
        P("spec"),
        P("spec", None),
        P(None, "wave"),
    )
    out_specs = (P(None, "wave"), P("spec", None))
    return jax.shard_map(
        functools.partial(shards, mesh.shape["spec"], mesh.shape["wave"]),
        mesh=mesh,
        in_specs=in_specs,
        out_specs=out_specs,
        check_vma=False,
    )
```

time: 841 us -> 326 us (0.39); the launches traced: 829 us -> 325 us
  waiting for transfers between devices: 690 us -> 0 us
  Pallas kernels: 0 us -> 315 us
  matrix products: 77.2 us -> 0 us
  local copies, waits for them, and re-layouts: 33.4 us -> 7.22 us
  between operations: 14.4 us -> 0.72 us
  other arithmetic: 12.9 us -> 1.46 us
    psum x8 -> x0, waiting for transfers between devices: 443 us -> none  [the longest x4 246 us: template_update(): num_a, den_a = lax.psum((num_t, den_t), 'spec')]
    pallas_call x0 -> x2, Pallas kernels: none -> 315 us  [the longest x1 312 us: shards(): pl.pallas_call(functools.partial(main_kernel, n_spec, n_wave), out_shape=...]
    all_gather x1 -> x0, waiting for transfers between devices: 246 us -> none  [shards(): whole = lax.all_gather(spectra, 'wave', axis=1, tiled=True)]
    dot_general x16 -> x0, matrix products: 77.2 us -> none  [the longest x8 42.7 us: over_rows(): lax.dot_general(left, right, (((0,), (0,)), ((), ())), preferred_element_...]
    gather x12 -> x0, local copies, waits for them, and re-layouts: 17.9 us -> none
    concatenate x1 -> x0, local copies, waits for them, and re-layouts: 13.1 us -> none  [shards(): jnp.concatenate([whole, jnp.zeros((rows, width), whole.dtype)], axis=1)]
    div x8 -> x0, other arithmetic: 12.2 us -> none  [the longest x4 6.33 us: template_update(): return temps * num_a / jnp.maximum(den_a, 1.0)]
  transfers between devices with their start and end apart: 9 -> 0, of which waited for: 9 -> 0; matrix products, arithmetic and copies ran while one was open for 1% -> 0% of each run, Pallas kernels for 0% -> 0%
where the time goes in v1:
time: 326 us; the launch traced here: 325 us
  Pallas kernels  315 us (97%)
  local copies, waits for them, and re-layouts  7.22 us (2%)
    pallas_call x1, Pallas kernels, shards(): pl.pallas_call(functools.partial(main_kernel, n_spec, n_wave), out_shape=...  312 us

profile of v1, /device:TPU:24, one launch (start us, length us, event | category | flops | bytes accessed | tf_op | source)
XLA Modules:
  0.0 324.9 jit_solution(17331596400421077617)
XLA Ops:
  0.6 0.0 copy-start
  0.7 0.8 and_select_fusion
  1.4 0.1 broadcast_bitcast_fusion
  1.5 0.7 broadcast_bitcast_fusion.1
  2.2 0.7 fusion.1
  2.9 0.0 copy-done
  2.9 0.2 broadcast_in_dim.16.lo_ref
  3.1 0.2 broadcast_in_dim.14.lo_ref
  3.3 0.2 broadcast_in_dim.15.hi_ref
  3.5 0.2 broadcast_in_dim.17.hi_ref
  3.7 0.0 copy-start.2
  3.8 2.0 copy-done.2
  5.8 0.0 copy-start.3
  5.8 3.3 %shard_map.77.rest_ref = bf16[1024,1920]{1,0:T(8,128)(2,1)S(1)} custom-call(s32[4]{0:T(128)S(1)} %get-tuple-element.3.shift_ref, bf16[1024,1792]{1,0:T(8,128)(2,1)S(1)} %copy-done.2, s32[1024,128]{1,0:T(8,128)S(1)} %broadcast_in_dim.14.lo_ref, s32[1024,128]{1,0:T(8,128)S(1)} %broadcast_in_dim.15.hi_ref), custom_call_target="tpu_custom_call" | custom-call | tf_op jit(solution)/shard_map/pallas_call | solution.py:38
  9.1 0.0 copy-start.1
  9.2 1.9 copy-done.1
  11.0 0.0 copy-done.3
  11.0 312.1 %shard_map.78 = (f32[128,1792]{1,0:T(8,128)S(1)}, f32[1024,128]{1,0:T(8,128)S(1)}) custom-call(s32[4]{0:T(128)S(1)} %get-tuple-element.2.first_ref, bf16[1024,1920]{1,0:T(8,128)(2,1)} %copy-done.1, s32[1024,128]{1,0:T(8,128)S(1)} %broadcast_in_dim.16.lo_ref, s32[1024,128]{1,0:T(8,128)S(1)} %broadcast_in_dim.17.hi_ref, f32[1024,128]{1,0:T(8,128)S(1)} %copy-done.3, ...), custom_call_target="tpu_custom_call" | custom-call | tf_op jit(solution)/shard_map/pallas_call | solution.py:450
  323.2 0.9 copy.15
  324.1 0.8 copy.16
  (3 shorter events, 0.0 us)
Async XLA Ops:
  0.6 2.3 copy-start
  3.7 2.0 copy-start.2
  5.8 5.2 %copy-start.3 = (f32[1024,128]{1,0:T(8,128)S(1)}, f32[1024,128]{1,0:T(8,128)}, u32[]{:S(2)}) copy-start(f32[1024,128]{1,0:T(8,128)} %coef_ref.1) | copy-start | bytes 1572868
  9.1 1.9 copy-start.1

commit v2 on v1

--- a/solution.py
+++ b/solution.py
@@ -74,10 +74,17 @@
     recv_a,
     send_b,
     recv_b,
+    wide_b,
+    recv_wb,
+    keep_b,
     send_z,
     recv_z,
-    stat_c,
+    send_c,
     recv_c,
+    wide_c,
+    recv_wc,
+    keep_c,
+    den_c,
     s_a,
     r_a,
     s_b,
@@ -115,6 +122,9 @@
     rank = n_spec * rank_part
     spans = rest_ref.shape[1] // LANES
     group = max(g for g in range(1, 6) if spans % g == 0)
+    some = max(g for g in range(1, 8) if chunk % g == 0)
+    unit = min(own, per)
+    units = rows // unit
     own_rows = pl.ds(pl.multiple_of(wave * own, own), own)
 
     def to_chip(k):
@@ -147,7 +157,7 @@
         pl.semaphore_signal(barrier, inc=1, device_id=to_wave(k), device_id_type=MESH)
     pl.semaphore_wait(barrier, n_spec + n_wave - 2)
 
-    def gather_templates():
+    def gather_templates(arrived=None):
         over_z = [None] + [
             copy(wbuf.at[spec, part_of(0)], wbuf.at[spec, part_of(0)], s_w.at[k], r_w.at[k], to_wave(k))
             for k in range(1, n_wave)
@@ -169,13 +179,19 @@
             for k in range(1, chips):
                 over_chips[kz, k].start()
             over_core[kz, 0].start()
-        for kz in range(n_wave):
-            for k in range(1, chips):
-                over_chips[kz, k].wait_recv()
-                over_core[kz, k].start()
+        for kz in range(n_wave + 1):
+            if kz < n_wave:
+                for k in range(1, chips):
+                    over_chips[kz, k].wait_recv()
+                    over_core[kz, k].start()
+            if kz:
+                for k in range(chips):
+                    over_core[kz - 1, k].wait_recv()
+                if arrived is not None:
+                    arrived(kz - 1)
         for kz in range(n_wave):
             for k in range(chips):
-                over_core[kz, k].wait()
+                over_core[kz, k].wait_send()
                 if k:
                     over_chips[kz, k].wait_send()
             if kz:
@@ -187,15 +203,24 @@
             return piece.astype(F32).reshape(rank, LANES).astype(BF16)
         return piece.reshape(rank, LANES)
 
-    def ratio_of(block, g):
-        at = pl.ds(pl.multiple_of(block * per, per), per)
-        start = first_ref[block] + g * group
+    def rows_of(at):
+        return pl.ds(pl.multiple_of(at * unit, unit), unit)
+
+    def ratio_of(at, g):
+        start = first_ref[at * unit // per] + g * group
         temps = jnp.concatenate(
             [tile_of(jnp.clip(start + k, 0, tiles - 1)) for k in range(group)], axis=1
         )
-        model = jnp.dot(hb[at, :], temps, preferred_element_type=F32)
-        rest = rest_ref[at, g * group * LANES : (g + 1) * group * LANES].astype(F32)
+        model = jnp.dot(hb[rows_of(at), :], temps, preferred_element_type=F32)
+        rest = rest_ref[rows_of(at), g * group * LANES : (g + 1) * group * LANES].astype(F32)
         return temps, jnp.where(rest > 0, rest / model, 0.0).astype(BF16)
+
+    def rounded(value, share):
+        wanted = value * share
+        sent = wanted.astype(BF16)
+        back = sent.astype(F32)
+        left = jnp.where(back > 0, wanted / back, 1.0)
+        return sent, jnp.clip(left, 0.99, 1.01)
 
     def put_stat(index, value):
         for part in range(n_spec):
@@ -205,13 +230,23 @@
         pixel = lax.broadcasted_iota(jnp.int32, low.shape, 1) + first
         return jnp.where((pixel >= low) & (pixel < high), 1.0, 0.0).astype(BF16)
 
+    def coef_copies():
+        return [
+            copy(hb.at[own_rows], hb.at[own_rows], s_h.at[k], r_h.at[k], to_wave(k))
+            for k in range(1, n_wave)
+        ]
+
     wown[...] = temp_ref[...]
     wbuf[spec, part_of(0)] = temp_ref[...].astype(BF16)
-    hb[...] = coef_ref[...].astype(BF16)
+    hb[own_rows, :] = coef_ref[own_rows, :].astype(BF16)
     hown[...] = coef_ref[own_rows, :]
-    for block in range(blocks):
-        parts[block, 0] = jnp.zeros((rank, LANES), F32)
-        parts[block, spans + 1] = jnp.zeros((rank, LANES), F32)
+    for one in coef_copies():
+        one.start()
+    for at in range(units):
+        parts[at, 0] = jnp.zeros((rank, LANES), F32)
+        parts[at, spans + 1] = jnp.zeros((rank, LANES), F32)
+    keep_b[...] = jnp.ones_like(keep_b)
+    keep_c[...] = jnp.ones_like(keep_c)
     gather_templates()
 
     last_temps = [
@@ -219,19 +254,23 @@
     ]
     order = list(range(1, n_wave)) + [0]
 
-    def update(step, unused):
-        def block_stats(block, unused):
-            at = pl.ds(pl.multiple_of(block * per, per), per)
-            for g in range(spans // group):
-                temps, ratio = ratio_of(block, g)
-                num = lax.dot_general(
-                    hb[at, :], ratio, (((0,), (0,)), ((), ())), preferred_element_type=F32
-                )
-                for k in range(group):
-                    parts[block, 1 + g * group + k] = num[:, k * LANES : (k + 1) * LANES]
-            return 0
-
-        lax.fori_loop(0, blocks, block_stats, 0)
+    def update(last):
+        out_b, in_b = (wide_b, recv_wb) if last else (send_b, recv_b)
+        out_c, in_c = (wide_c, recv_wc) if last else (send_c, recv_c)
+
+        copies_h = coef_copies()
+        for kz in range(n_wave):
+            if kz:
+                copies_h[kz - 1].wait()
+            for j in range(own // unit):
+                at = lax.rem(wave + n_wave - kz, n_wave) * (own // unit) + j
+                for g in range(spans // group):
+                    temps, ratio = ratio_of(at, g)
+                    num = lax.dot_general(
+                        hb[rows_of(at), :], ratio, (((0,), (0,)), ((), ())), preferred_element_type=F32
+                    )
+                    for k in range(group):
+                        parts[at, 1 + g * group + k] = num[:, k * LANES : (k + 1) * LANES]
 
         copies_a = {}
         copies_b = {}
@@ -241,15 +280,12 @@
                 send_a.at[buddy, :, where], recv_a.at[:, where], s_a.at[kz], r_a.at[kz], to_buddy()
             )
             for k in range(1, chips):
+                source, target = (out_b, in_b) if kz < n_wave else (wide_b, recv_wb)
                 copies_b[kz, k] = copy(
-                    send_b.at[lax.rem(chip + k, chips), where],
-                    recv_b.at[k - 1, where],
-                    s_b.at[kz, k],
-                    r_b.at[kz, k],
-                    to_chip(k),
+                    source.at[k - 1, where], target.at[k - 1, where], s_b.at[kz, k], r_b.at[kz, k], to_chip(k)
                 )
         copies_z = {
-            k: copy(send_z.at[part_of(k)], recv_z.at[k - 1], s_z.at[k], r_z.at[k], to_wave(k))
+            k: copy(send_z.at[k - 1], recv_z.at[k - 1], s_z.at[k], r_z.at[k], to_wave(k))
             for k in range(1, n_wave)
         }
 
@@ -258,9 +294,10 @@
 
             def add_blocks(i, unused):
                 index = first + i
-                total = parts[0, jnp.clip(index - first_ref[0], -1, spans) + 1]
-                for block in range(1, blocks):
-                    total = total + parts[block, jnp.clip(index - first_ref[block], -1, spans) + 1]
+                total = None
+                for at in range(units):
+                    place = jnp.clip(index - first_ref[at * unit // per], -1, spans) + 1
+                    total = parts[at, place] if at == 0 else total + parts[at, place]
                 put_stat(index, total)
                 return 0
 
@@ -283,20 +320,26 @@
             copies_a[kz].wait_recv()
 
             def add_core(i, unused):
-                for c in range(chips):
-                    send_b[c, first + i] = (
-                        send_a[core, c, first + i] + recv_a[c, first + i]
-                    ).astype(send_b.dtype)
+                index = first + i
+                for k in range(1, chips):
+                    c = lax.rem(chip + k, chips)
+                    value = send_a[core, c, index] + recv_a[c, index]
+                    if kz == n_wave:
+                        wide_b[k - 1, index] = value
+                    elif last:
+                        out_b[k - 1, index] = value * keep_b[k - 1, index]
+                    else:
+                        out_b[k - 1, index], keep_b[k - 1, index] = rounded(value, keep_b[k - 1, index])
                 return 0
 
             lax.fori_loop(0, chunk, add_core, 0)
             for k in range(1, chips):
                 copies_b[kz, k].start()
 
-        def chip_sum(index):
+        def chip_sum(index, landed=in_b):
             total = send_a[core, chip, index] + recv_a[chip, index]
             for k in range(1, chips):
-                total = total + recv_b[k - 1, index].astype(F32)
+                total = total + landed[k - 1, index].astype(F32)
             return total
 
         for kz in order[:-1]:
@@ -305,7 +348,7 @@
                 copies_b[kz, k].wait_recv()
 
             def add_chips(i, unused):
-                send_z[first + i] = chip_sum(first + i)
+                send_z[kz - 1, i] = chip_sum(first + i)
                 return 0
 
             lax.fori_loop(0, chunk, add_chips, 0)
@@ -320,7 +363,7 @@
             num = chip_sum(wave * chunk + i)
             for k in range(1, n_wave):
                 num = num + recv_z[k - 1, i]
-            value = wown[i] * num / jnp.maximum(chip_sum(tiles + i), 1.0)
+            value = wown[i] * num / jnp.maximum(chip_sum(tiles + i, recv_wb), 1.0)
             wown[i] = value
             wbuf[spec, wave * chunk + i] = value.astype(BF16)
             return 0
@@ -333,73 +376,78 @@
         for k in range(1, n_wave):
             copies_z[k].wait_send()
 
-        gather_templates()
-
-        @pl.when(step == ITERS - 1)
-        def _():
+        den_c[...] = jnp.zeros_like(den_c)
+
+        def add_den(kz):
+            first = lax.rem(wave + n_wave - kz, n_wave) * chunk
+
+            def some_tiles(i, unused):
+                index = first + i * some
+                masks = [
+                    mask_of(lo_ref[own_rows, :], hi_ref[own_rows, :], (index + k) * LANES)
+                    for k in range(some)
+                ]
+                den_c[...] += lax.dot_general(
+                    jnp.concatenate(masks, axis=1),
+                    jnp.concatenate([tile_of(index + k) for k in range(some)], axis=1),
+                    (((1,), (1,)), ((), ())),
+                    preferred_element_type=F32,
+                )
+                return 0
+
+            lax.fori_loop(0, chunk // some, some_tiles, 0)
+
+        gather_templates(add_den)
+
+        if last:
             for one in last_temps:
                 one.start()
 
-        def block_coefs(block, unused):
-            at = pl.ds(pl.multiple_of(block * per, per), per)
-            total = jnp.zeros((per, rank), F32)
-            for g in range(spans // group):
-                temps, ratio = ratio_of(block, g)
-                total = total + lax.dot_general(
-                    ratio, temps, (((1,), (1,)), ((), ())), preferred_element_type=F32
-                )
-            stat_c[at, :] = total
-            return 0
-
-        lax.fori_loop(0, blocks, block_coefs, 0)
-        copies_c = []
-        for k in range(1, n_wave):
-            theirs = pl.ds(pl.multiple_of(lax.rem(wave + k, n_wave) * own, own), own)
-            copies_c.append(
-                copy(stat_c.at[theirs], recv_c.at[k - 1], s_c.at[k], r_c.at[k], to_wave(k))
-            )
-        for one in copies_c:
-            one.start()
-
-        def den_coef(i, total):
-            masks = []
-            temps = []
-            for k in range(4):
-                masks.append(mask_of(lo_ref[own_rows, :], hi_ref[own_rows, :], (i * 4 + k) * LANES))
-                temps.append(tile_of(i * 4 + k))
-            return total + lax.dot_general(
-                jnp.concatenate(masks, axis=1),
-                jnp.concatenate(temps, axis=1),
-                (((1,), (1,)), ((), ())),
-                preferred_element_type=F32,
-            )
-
-        den = lax.fori_loop(0, tiles // 4, den_coef, jnp.zeros((own, rank), F32))
+        copies_c = [
+            copy(out_c.at[k - 1], in_c.at[k - 1], s_c.at[k], r_c.at[k], to_wave(k))
+            for k in range(1, n_wave)
+        ]
+        mine = None
+        for kz in order:
+            pieces = []
+            for j in range(own // unit):
+                at = lax.rem(wave + kz, n_wave) * (own // unit) + j
+                total = None
+                for g in range(spans // group):
+                    temps, ratio = ratio_of(at, g)
+                    num = lax.dot_general(
+                        ratio, temps, (((1,), (1,)), ((), ())), preferred_element_type=F32
+                    )
+                    total = num if g == 0 else total + num
+                pieces.append(total)
+            total = pieces[0] if len(pieces) == 1 else jnp.concatenate(pieces, axis=0)
+            if kz == 0:
+                mine = total
+            else:
+                if last:
+                    out_c[kz - 1] = total * keep_c[kz - 1]
+                else:
+                    out_c[kz - 1], keep_c[kz - 1] = rounded(total, keep_c[kz - 1])
+                copies_c[kz - 1].start()
         for one in copies_c:
             one.wait_recv()
-        num = stat_c[own_rows, :]
         for k in range(1, n_wave):
-            num = num + recv_c[k - 1]
-        value = hown[...] * num / jnp.maximum(den, 1.0)
+            mine = mine + in_c[k - 1].astype(F32)
+        value = hown[...] * mine / jnp.maximum(den_c[...], 1.0)
         hown[...] = value
         for one in copies_c:
             one.wait_send()
-
-        @pl.when(step < ITERS - 1)
-        def _():
+        if not last:
             hb[own_rows, :] = value.astype(BF16)
-            copies_h = [
-                copy(hb.at[own_rows], hb.at[own_rows], s_h.at[k], r_h.at[k], to_wave(k))
-                for k in range(1, n_wave)
-            ]
-            for one in copies_h:
+            for one in coef_copies():
                 one.start()
-            for one in copies_h:
-                one.wait()
-
+
+    def step(i, unused):
+        update(False)
         return 0
 
-    lax.fori_loop(0, ITERS, update, 0)
+    lax.fori_loop(0, ITERS - 1, step, 0)
+    update(True)
 
     last_coefs = [
         copy(hown, hfin.at[wave], s_g.at[k], r_g.at[k], to_wave(k)) for k in range(1, n_wave)
@@ -462,15 +510,22 @@
             pltpu.VMEM((rows, rank), BF16),
             pltpu.VMEM((own, rank), F32),
             pltpu.VMEM((n_wave, own, rank), F32),
-            pltpu.VMEM((blocks, chunk + 3, rank, LANES), F32),
+            pltpu.VMEM((rows // min(own, rows // blocks), chunk + 3, rank, LANES), F32),
             pltpu.VMEM((2, chips, tiles + chunk, part, LANES), F32),
             pltpu.VMEM((chips, tiles + chunk, part, LANES), F32),
-            pltpu.VMEM((chips, tiles + chunk, part, LANES), F32),
+            pltpu.VMEM((chips - 1, tiles + chunk, part, LANES), BF16),
+            pltpu.VMEM((chips - 1, tiles + chunk, part, LANES), BF16),
             pltpu.VMEM((chips - 1, tiles + chunk, part, LANES), F32),
-            pltpu.VMEM((tiles, part, LANES), F32),
+            pltpu.VMEM((chips - 1, tiles + chunk, part, LANES), F32),
+            pltpu.VMEM((chips - 1, tiles + chunk, part, LANES), F32),
             pltpu.VMEM((n_wave - 1, chunk, part, LANES), F32),
-            pltpu.VMEM((rows, rank), F32),
+            pltpu.VMEM((n_wave - 1, chunk, part, LANES), F32),
+            pltpu.VMEM((n_wave - 1, own, rank), BF16),
+            pltpu.VMEM((n_wave - 1, own, rank), BF16),
             pltpu.VMEM((n_wave - 1, own, rank), F32),
+            pltpu.VMEM((n_wave - 1, own, rank), F32),
+            pltpu.VMEM((n_wave - 1, own, rank), F32),
+            pltpu.VMEM((own, rank), F32),
         ]
         + [dma((n_wave + 1,))] * 2
         + [dma((n_wave + 1, chips))] * 2

time: 326 us -> 281 us (0.86)
  Pallas kernels: 315 us -> 271 us
    pallas_call x1, Pallas kernels: 312 us -> 268 us  [shards(): pl.pallas_call(functools.partial(main_kernel, n_spec, n_wave), out_shape=...]
where the time goes in v2:
time: 281 us; the launch traced here: 280 us
  Pallas kernels  271 us (96%)
  local copies, waits for them, and re-layouts  7.22 us (3%)
    pallas_call x1, Pallas kernels, shards(): pl.pallas_call(functools.partial(main_kernel, n_spec, n_wave), out_shape=...  268 us
    unnamed x14, local copies, waits for them, and re-layouts  6.44 us

profile of v2, /device:TPU:24, one launch (start us, length us, event | category | flops | bytes accessed | tf_op | source)
XLA Modules:
  0.0 280.3 jit_solution(10699504853434251461)
XLA Ops:
  0.6 0.0 copy-start
  0.7 0.8 and_select_fusion
  1.4 0.1 broadcast_bitcast_fusion
  1.5 0.7 broadcast_bitcast_fusion.1
  2.2 0.7 fusion.1
  2.9 0.0 copy-done
  2.9 0.2 broadcast_in_dim.16.lo_ref
  3.1 0.2 broadcast_in_dim.14.lo_ref
  3.3 0.2 broadcast_in_dim.15.hi_ref
  3.5 0.2 broadcast_in_dim.17.hi_ref
  3.7 0.0 copy-start.2
  3.8 2.0 copy-done.2
  5.8 0.0 copy-start.3
  5.8 3.3 %shard_map.77.rest_ref = bf16[1024,1920]{1,0:T(8,128)(2,1)S(1)} custom-call(s32[4]{0:T(128)S(1)} %get-tuple-element.3.shift_ref, bf16[1024,1792]{1,0:T(8,128)(2,1)S(1)} %copy-done.2, s32[1024,128]{1,0:T(8,128)S(1)} %broadcast_in_dim.14.lo_ref, s32[1024,128]{1,0:T(8,128)S(1)} %broadcast_in_dim.15.hi_ref), custom_call_target="tpu_custom_call" | custom-call | tf_op jit(solution)/shard_map/pallas_call | solution.py:38
  9.1 0.0 copy-start.1
  9.2 1.9 copy-done.1
  11.0 0.0 copy-done.3
  11.0 267.5 %shard_map.78 = (f32[128,1792]{1,0:T(8,128)S(1)}, f32[1024,128]{1,0:T(8,128)S(1)}) custom-call(s32[4]{0:T(128)S(1)} %get-tuple-element.2.first_ref, bf16[1024,1920]{1,0:T(8,128)(2,1)} %copy-done.1, s32[1024,128]{1,0:T(8,128)S(1)} %broadcast_in_dim.16.lo_ref, s32[1024,128]{1,0:T(8,128)S(1)} %broadcast_in_dim.17.hi_ref, f32[1024,128]{1,0:T(8,128)S(1)} %copy-done.3, ...), custom_call_target="tpu_custom_call" | custom-call | tf_op jit(solution)/shard_map/pallas_call | solution.py:498
  278.6 0.9 copy.15
  279.5 0.8 copy.16
  (3 shorter events, 0.0 us)
Async XLA Ops:
  0.6 2.3 copy-start
  3.7 2.0 copy-start.2
  5.8 5.2 %copy-start.3 = (f32[1024,128]{1,0:T(8,128)S(1)}, f32[1024,128]{1,0:T(8,128)}, u32[]{:S(2)}) copy-start(f32[1024,128]{1,0:T(8,128)} %coef_ref.1) | copy-start | bytes 1572868
  9.1 1.9 copy-start.1

commit v3 on v2

--- a/solution.py
+++ b/solution.py
@@ -85,6 +85,7 @@
     recv_wc,
     keep_c,
     den_c,
+    den_t,
     s_a,
     r_a,
     s_b,
@@ -127,8 +128,16 @@
     units = rows // unit
     own_rows = pl.ds(pl.multiple_of(wave * own, own), own)
 
+    def chip_at(k):
+        if chips == 4:
+            return [chip, chip + 1 - 2 * (chip % 2), lax.rem(chip + 2, 4), 3 - chip][k]
+        return lax.rem(chip + k, chips)
+
+    def chip_from(k):
+        return chip_at(k) if chips == 4 else lax.rem(chip + chips - k, chips)
+
     def to_chip(k):
-        return (lax.rem(chip + k, chips) * 2 + core, wave)
+        return (chip_at(k) * 2 + core, wave)
 
     def to_buddy():
         return (chip * 2 + buddy, wave)
@@ -166,29 +175,46 @@
         over_core = {}
         for kz in range(n_wave):
             for k in range(chips):
-                slot = wbuf.at[lax.rem(chip + chips - k, chips) * 2 + core, part_from(kz)]
+                slot = wbuf.at[chip_from(k) * 2 + core, part_from(kz)]
                 over_core[kz, k] = copy(slot, slot, s_wc.at[kz, k], r_wc.at[kz, k], to_buddy())
-                if k:
+                if chips == 4 and k == 3:
+                    slot = wbuf.at[chip_at(1 + kz % 2) * 2 + core, part_from(kz)]
+                    over_chips[kz, k] = copy(
+                        slot, slot, s_wb.at[kz, k], r_wb.at[kz, k], to_chip(2 - kz % 2)
+                    )
+                elif k:
                     mine = wbuf.at[spec, part_from(kz)]
                     over_chips[kz, k] = copy(mine, mine, s_wb.at[kz, k], r_wb.at[kz, k], to_chip(k))
+        direct = range(1, 3) if chips == 4 else range(1, chips)
+        relayed = range(3, 4) if chips == 4 else ()
         for k in range(1, n_wave):
             over_z[k].start()
-        for kz in range(n_wave):
-            if kz:
-                over_z[kz].wait_recv()
-            for k in range(1, chips):
-                over_chips[kz, k].start()
-            over_core[kz, 0].start()
-        for kz in range(n_wave + 1):
-            if kz < n_wave:
-                for k in range(1, chips):
+        for stage in range(n_wave + 3):
+            if stage < n_wave:
+                if stage:
+                    over_z[stage].wait_recv()
+                for k in direct:
+                    over_chips[stage, k].start()
+                over_core[stage, 0].start()
+            if 1 <= stage <= n_wave:
+                kz = stage - 1
+                for k in direct:
+                    over_chips[kz, k].wait_recv()
+                    for other in relayed:
+                        if k == 1 + kz % 2:
+                            over_chips[kz, other].start()
+                    over_core[kz, k].start()
+            if 2 <= stage <= n_wave + 1:
+                kz = stage - 2
+                for k in relayed:
                     over_chips[kz, k].wait_recv()
                     over_core[kz, k].start()
-            if kz:
+            if stage >= 3:
+                kz = stage - 3
                 for k in range(chips):
-                    over_core[kz - 1, k].wait_recv()
+                    over_core[kz, k].wait_recv()
                 if arrived is not None:
-                    arrived(kz - 1)
+                    arrived(kz)
         for kz in range(n_wave):
             for k in range(chips):
                 over_core[kz, k].wait_send()
@@ -213,14 +239,16 @@
         )
         model = jnp.dot(hb[rows_of(at), :], temps, preferred_element_type=F32)
         rest = rest_ref[rows_of(at), g * group * LANES : (g + 1) * group * LANES].astype(F32)
-        return temps, jnp.where(rest > 0, rest / model, 0.0).astype(BF16)
-
-    def rounded(value, share):
+        inverse = pl.reciprocal(model, approx=True)
+        inverse = inverse * (2.0 - model * inverse)
+        return temps, jnp.where(rest > 0, rest * inverse, 0.0).astype(BF16)
+
+    def change_of(value, share, held):
         wanted = value * share
-        sent = wanted.astype(BF16)
-        back = sent.astype(F32)
-        left = jnp.where(back > 0, wanted / back, 1.0)
-        return sent, jnp.clip(left, 0.99, 1.01)
+        sent = (wanted - held).astype(BF16)
+        held = held + sent.astype(F32)
+        left = jnp.where(held > 0, wanted / held, 1.0)
+        return sent, held, jnp.clip(left, 0.99, 1.01)
 
     def put_stat(index, value):
         for part in range(n_spec):
@@ -254,23 +282,9 @@
     ]
     order = list(range(1, n_wave)) + [0]
 
-    def update(last):
-        out_b, in_b = (wide_b, recv_wb) if last else (send_b, recv_b)
-        out_c, in_c = (wide_c, recv_wc) if last else (send_c, recv_c)
-
-        copies_h = coef_copies()
-        for kz in range(n_wave):
-            if kz:
-                copies_h[kz - 1].wait()
-            for j in range(own // unit):
-                at = lax.rem(wave + n_wave - kz, n_wave) * (own // unit) + j
-                for g in range(spans // group):
-                    temps, ratio = ratio_of(at, g)
-                    num = lax.dot_general(
-                        hb[rows_of(at), :], ratio, (((0,), (0,)), ((), ())), preferred_element_type=F32
-                    )
-                    for k in range(group):
-                        parts[at, 1 + g * group + k] = num[:, k * LANES : (k + 1) * LANES]
+    def update(opening, step):
+        out_b, in_b = (wide_b, recv_wb) if opening else (send_b, recv_b)
+        out_c, in_c = (wide_c, recv_wc) if opening else (send_c, recv_c)
 
         copies_a = {}
         copies_b = {}
@@ -289,6 +303,76 @@
             for k in range(1, n_wave)
         }
 
+        def send_sums(kz):
+            first = lax.rem(wave + kz, n_wave) * chunk if kz < n_wave else tiles
+            copies_a[kz].wait_recv()
+
+            def add_core(i, unused):
+                index = first + i
+                for k in range(1, chips):
+                    c = chip_at(k)
+                    value = send_a[core, c, index] + recv_a[c, index]
+                    if kz == n_wave or opening:
+                        wide_b[k - 1, index] = value
+                    else:
+                        send_b[k - 1, index], wide_b[k - 1, index], keep_b[k - 1, index] = change_of(
+                            value, keep_b[k - 1, index], wide_b[k - 1, index]
+                        )
+                return 0
+
+            lax.fori_loop(0, chunk, add_core, 0)
+            for k in range(1, chips):
+                copies_b[kz, k].start()
+
+        copies_h = coef_copies()
+        for kz in range(n_wave):
+            if kz:
+                copies_h[kz - 1].wait()
+            for j in range(own // unit):
+                at = lax.rem(wave + n_wave - kz, n_wave) * (own // unit) + j
+
+                def some_dens(i, unused):
+                    index = i * some
+                    masks = [
+                        mask_of(
+                            lo_ref[rows_of(at), :],
+                            hi_ref[rows_of(at), :],
+                            (wave * chunk + index + k) * LANES,
+                        )
+                        for k in range(some)
+                    ]
+                    den = lax.dot_general(
+                        hb[rows_of(at), :],
+                        jnp.concatenate(masks, axis=1),
+                        (((0,), (0,)), ((), ())),
+                        preferred_element_type=F32,
+                    )
+                    for k in range(some):
+                        piece = den[:, k * LANES : (k + 1) * LANES]
+                        if kz == 0 and j == 0:
+                            den_t[index + k] = piece
+                        else:
+                            den_t[index + k] += piece
+                    return 0
+
+                lax.fori_loop(0, chunk // some, some_dens, 0)
+                if kz == n_wave - 1 and j == own // unit - 1:
+
+                    def put_den(i, unused):
+                        put_stat(tiles + i, den_t[i])
+                        return 0
+
+                    lax.fori_loop(0, chunk, put_den, 0)
+                    copies_a[n_wave].start()
+                for g in range(spans // group):
+                    temps, ratio = ratio_of(at, g)
+                    num = lax.dot_general(
+                        hb[rows_of(at), :], ratio, (((0,), (0,)), ((), ())), preferred_element_type=F32
+                    )
+                    for k in range(group):
+                        parts[at, 1 + g * group + k] = num[:, k * LANES : (k + 1) * LANES]
+        send_sums(n_wave)
+
         for kz in order:
             first = lax.rem(wave + kz, n_wave) * chunk
 
@@ -304,42 +388,17 @@
             lax.fori_loop(0, chunk, add_blocks, 0)
             copies_a[kz].start()
 
-        def den_tile(i, unused):
-            mask = mask_of(lo_ref[...], hi_ref[...], (wave * chunk + i) * LANES)
-            put_stat(
-                tiles + i,
-                lax.dot_general(hb[...], mask, (((0,), (0,)), ((), ())), preferred_element_type=F32),
-            )
-            return 0
-
-        lax.fori_loop(0, chunk, den_tile, 0)
-        copies_a[n_wave].start()
-
-        for kz in order + [n_wave]:
-            first = lax.rem(wave + kz, n_wave) * chunk if kz < n_wave else tiles
-            copies_a[kz].wait_recv()
-
-            def add_core(i, unused):
-                index = first + i
-                for k in range(1, chips):
-                    c = lax.rem(chip + k, chips)
-                    value = send_a[core, c, index] + recv_a[c, index]
-                    if kz == n_wave:
-                        wide_b[k - 1, index] = value
-                    elif last:
-                        out_b[k - 1, index] = value * keep_b[k - 1, index]
-                    else:
-                        out_b[k - 1, index], keep_b[k - 1, index] = rounded(value, keep_b[k - 1, index])
-                return 0
-
-            lax.fori_loop(0, chunk, add_core, 0)
-            for k in range(1, chips):
-                copies_b[kz, k].start()
-
-        def chip_sum(index, landed=in_b):
+        for kz in order:
+            send_sums(kz)
+
+        def chip_sum(index, den=False):
             total = send_a[core, chip, index] + recv_a[chip, index]
             for k in range(1, chips):
-                total = total + landed[k - 1, index].astype(F32)
+                landed = recv_wb[k - 1, index]
+                if not (opening or den):
+                    landed = landed + recv_b[k - 1, index].astype(F32)
+                    recv_wb[k - 1, index] = landed
+                total = total + landed
             return total
 
         for kz in order[:-1]:
@@ -363,7 +422,7 @@
             num = chip_sum(wave * chunk + i)
             for k in range(1, n_wave):
                 num = num + recv_z[k - 1, i]
-            value = wown[i] * num / jnp.maximum(chip_sum(tiles + i, recv_wb), 1.0)
+            value = wown[i] * num / jnp.maximum(chip_sum(tiles + i, True), 1.0)
             wown[i] = value
             wbuf[spec, wave * chunk + i] = value.astype(BF16)
             return 0
@@ -399,9 +458,12 @@
 
         gather_templates(add_den)
 
-        if last:
-            for one in last_temps:
-                one.start()
+        if not opening:
+
+            @pl.when(step == ITERS - 1)
+            def _():
+                for one in last_temps:
+                    one.start()
 
         copies_c = [
             copy(out_c.at[k - 1], in_c.at[k - 1], s_c.at[k], r_c.at[k], to_wave(k))
@@ -424,30 +486,38 @@
             if kz == 0:
                 mine = total
             else:
-                if last:
-                    out_c[kz - 1] = total * keep_c[kz - 1]
+                if opening:
+                    wide_c[kz - 1] = total
                 else:
-                    out_c[kz - 1], keep_c[kz - 1] = rounded(total, keep_c[kz - 1])
+                    send_c[kz - 1], wide_c[kz - 1], keep_c[kz - 1] = change_of(
+                        total, keep_c[kz - 1], wide_c[kz - 1]
+                    )
                 copies_c[kz - 1].start()
         for one in copies_c:
             one.wait_recv()
         for k in range(1, n_wave):
-            mine = mine + in_c[k - 1].astype(F32)
+            landed = recv_wc[k - 1]
+            if not opening:
+                landed = landed + recv_c[k - 1].astype(F32)
+                recv_wc[k - 1] = landed
+            mine = mine + landed
         value = hown[...] * mine / jnp.maximum(den_c[...], 1.0)
         hown[...] = value
         for one in copies_c:
             one.wait_send()
-        if not last:
+
+        @pl.when(step < ITERS - 1)
+        def _():
             hb[own_rows, :] = value.astype(BF16)
             for one in coef_copies():
                 one.start()
 
-    def step(i, unused):
-        update(False)
+    def later(step, unused):
+        update(False, step)
         return 0
 
-    lax.fori_loop(0, ITERS - 1, step, 0)
-    update(True)
+    update(True, 0)
+    lax.fori_loop(1, ITERS, later, 0)
 
     last_coefs = [
         copy(hown, hfin.at[wave], s_g.at[k], r_g.at[k], to_wave(k)) for k in range(1, n_wave)
@@ -526,6 +596,7 @@
             pltpu.VMEM((n_wave - 1, own, rank), F32),
             pltpu.VMEM((n_wave - 1, own, rank), F32),
             pltpu.VMEM((own, rank), F32),
+            pltpu.VMEM((chunk, rank, LANES), F32),
         ]
         + [dma((n_wave + 1,))] * 2
         + [dma((n_wave + 1, chips))] * 2

time: 281 us -> 306 us (1.089)
  Pallas kernels: 271 us -> 296 us
    pallas_call x1, Pallas kernels: 268 us -> 292 us  [shards(): pl.pallas_call(functools.partial(main_kernel, n_spec, n_wave), out_shape=...]
where the time goes in v3:
time: 306 us; the launch traced here: 305 us
  Pallas kernels  296 us (97%)
  local copies, waits for them, and re-layouts  7.22 us (2%)
    pallas_call x1, Pallas kernels, shards(): pl.pallas_call(functools.partial(main_kernel, n_spec, n_wave), out_shape=...  292 us
    unnamed x14, local copies, waits for them, and re-layouts  6.44 us

profile of v3, /device:TPU:24, one launch (start us, length us, event | category | flops | bytes accessed | tf_op | source)
XLA Modules:
  0.0 305.0 jit_solution(1154967166186739326)
XLA Ops:
  0.6 0.0 copy-start
  0.7 0.8 and_select_fusion
  1.4 0.1 broadcast_bitcast_fusion
  1.5 0.7 broadcast_bitcast_fusion.1
  2.2 0.7 fusion.1
  2.9 0.0 copy-done
  2.9 0.2 broadcast_in_dim.16.lo_ref
  3.1 0.2 broadcast_in_dim.14.lo_ref
  3.3 0.2 broadcast_in_dim.15.hi_ref
  3.5 0.2 broadcast_in_dim.17.hi_ref
  3.7 0.0 copy-start.2
  3.8 2.0 copy-done.2
  5.8 0.0 copy-start.3
  5.8 3.3 %shard_map.77.rest_ref = bf16[1024,1920]{1,0:T(8,128)(2,1)S(1)} custom-call(s32[4]{0:T(128)S(1)} %get-tuple-element.3.shift_ref, bf16[1024,1792]{1,0:T(8,128)(2,1)S(1)} %copy-done.2, s32[1024,128]{1,0:T(8,128)S(1)} %broadcast_in_dim.14.lo_ref, s32[1024,128]{1,0:T(8,128)S(1)} %broadcast_in_dim.15.hi_ref), custom_call_target="tpu_custom_call" | custom-call | tf_op jit(solution)/shard_map/pallas_call | solution.py:38
  9.1 0.0 copy-start.1
  9.2 1.9 copy-done.1
  11.0 0.0 copy-done.3
  11.0 292.2 %shard_map.78 = (f32[128,1792]{1,0:T(8,128)S(1)}, f32[1024,128]{1,0:T(8,128)S(1)}) custom-call(s32[4]{0:T(128)S(1)} %get-tuple-element.2.first_ref, bf16[1024,1920]{1,0:T(8,128)(2,1)} %copy-done.1, s32[1024,128]{1,0:T(8,128)S(1)} %broadcast_in_dim.16.lo_ref, s32[1024,128]{1,0:T(8,128)S(1)} %broadcast_in_dim.17.hi_ref, f32[1024,128]{1,0:T(8,128)S(1)} %copy-done.3, ...), custom_call_target="tpu_custom_call" | custom-call | tf_op jit(solution)/shard_map/pallas_call | solution.py:568
  303.3 0.9 copy.15
  304.2 0.8 copy.16
  (3 shorter events, 0.0 us)
Async XLA Ops:
  0.6 2.3 copy-start
  3.7 2.0 copy-start.2
  5.8 5.2 %copy-start.3 = (f32[1024,128]{1,0:T(8,128)S(1)}, f32[1024,128]{1,0:T(8,128)}, u32[]{:S(2)}) copy-start(f32[1024,128]{1,0:T(8,128)} %coef_ref.1) | copy-start | bytes 1572868
  9.1 1.9 copy-start.1

commit v4 on v2

--- a/solution.py
+++ b/solution.py
@@ -215,12 +215,12 @@
         rest = rest_ref[rows_of(at), g * group * LANES : (g + 1) * group * LANES].astype(F32)
         return temps, jnp.where(rest > 0, rest / model, 0.0).astype(BF16)
 
-    def rounded(value, share):
+    def change_of(value, share, held):
         wanted = value * share
-        sent = wanted.astype(BF16)
-        back = sent.astype(F32)
-        left = jnp.where(back > 0, wanted / back, 1.0)
-        return sent, jnp.clip(left, 0.99, 1.01)
+        sent = (wanted - held).astype(BF16)
+        held = held + sent.astype(F32)
+        left = jnp.where(held > 0, wanted / held, 1.0)
+        return sent, held, jnp.clip(left, 0.99, 1.01)
 
     def put_stat(index, value):
         for part in range(n_spec):
@@ -254,9 +254,9 @@
     ]
     order = list(range(1, n_wave)) + [0]
 
-    def update(last):
-        out_b, in_b = (wide_b, recv_wb) if last else (send_b, recv_b)
-        out_c, in_c = (wide_c, recv_wc) if last else (send_c, recv_c)
+    def update(opening, step):
+        out_b, in_b = (wide_b, recv_wb) if opening else (send_b, recv_b)
+        out_c, in_c = (wide_c, recv_wc) if opening else (send_c, recv_c)
 
         copies_h = coef_copies()
         for kz in range(n_wave):
@@ -324,22 +324,26 @@
                 for k in range(1, chips):
                     c = lax.rem(chip + k, chips)
                     value = send_a[core, c, index] + recv_a[c, index]
-                    if kz == n_wave:
+                    if kz == n_wave or opening:
                         wide_b[k - 1, index] = value
-                    elif last:
-                        out_b[k - 1, index] = value * keep_b[k - 1, index]
                     else:
-                        out_b[k - 1, index], keep_b[k - 1, index] = rounded(value, keep_b[k - 1, index])
+                        send_b[k - 1, index], wide_b[k - 1, index], keep_b[k - 1, index] = change_of(
+                            value, keep_b[k - 1, index], wide_b[k - 1, index]
+                        )
                 return 0
 
             lax.fori_loop(0, chunk, add_core, 0)
             for k in range(1, chips):
                 copies_b[kz, k].start()
 
-        def chip_sum(index, landed=in_b):
+        def chip_sum(index, den=False):
             total = send_a[core, chip, index] + recv_a[chip, index]
             for k in range(1, chips):
-                total = total + landed[k - 1, index].astype(F32)
+                landed = recv_wb[k - 1, index]
+                if not (opening or den):
+                    landed = landed + recv_b[k - 1, index].astype(F32)
+                    recv_wb[k - 1, index] = landed
+                total = total + landed
             return total
 
         for kz in order[:-1]:
@@ -363,7 +367,7 @@
             num = chip_sum(wave * chunk + i)
             for k in range(1, n_wave):
                 num = num + recv_z[k - 1, i]
-            value = wown[i] * num / jnp.maximum(chip_sum(tiles + i, recv_wb), 1.0)
+            value = wown[i] * num / jnp.maximum(chip_sum(tiles + i, True), 1.0)
             wown[i] = value
             wbuf[spec, wave * chunk + i] = value.astype(BF16)
             return 0
@@ -399,9 +403,12 @@
 
         gather_templates(add_den)
 
-        if last:
-            for one in last_temps:
-                one.start()
+        if not opening:
+
+            @pl.when(step == ITERS - 1)
+            def _():
+                for one in last_temps:
+                    one.start()
 
         copies_c = [
             copy(out_c.at[k - 1], in_c.at[k - 1], s_c.at[k], r_c.at[k], to_wave(k))
@@ -424,30 +431,38 @@
             if kz == 0:
                 mine = total
             else:
-                if last:
-                    out_c[kz - 1] = total * keep_c[kz - 1]
+                if opening:
+                    wide_c[kz - 1] = total
                 else:
-                    out_c[kz - 1], keep_c[kz - 1] = rounded(total, keep_c[kz - 1])
+                    send_c[kz - 1], wide_c[kz - 1], keep_c[kz - 1] = change_of(
+                        total, keep_c[kz - 1], wide_c[kz - 1]
+                    )
                 copies_c[kz - 1].start()
         for one in copies_c:
             one.wait_recv()
         for k in range(1, n_wave):
-            mine = mine + in_c[k - 1].astype(F32)
+            landed = recv_wc[k - 1]
+            if not opening:
+                landed = landed + recv_c[k - 1].astype(F32)
+                recv_wc[k - 1] = landed
+            mine = mine + landed
         value = hown[...] * mine / jnp.maximum(den_c[...], 1.0)
         hown[...] = value
         for one in copies_c:
             one.wait_send()
-        if not last:
+
+        @pl.when(step < ITERS - 1)
+        def _():
             hb[own_rows, :] = value.astype(BF16)
             for one in coef_copies():
                 one.start()
 
-    def step(i, unused):
-        update(False)
+    def later(step, unused):
+        update(False, step)
         return 0
 
-    lax.fori_loop(0, ITERS - 1, step, 0)
-    update(True)
+    update(True, 0)
+    lax.fori_loop(1, ITERS, later, 0)
 
     last_coefs = [
         copy(hown, hfin.at[wave], s_g.at[k], r_g.at[k], to_wave(k)) for k in range(1, n_wave)

time: 281 us -> 281 us (level)
  no operation moved by 1% of the time
where the time goes in v4:
time: 281 us
  Pallas kernels  271 us (96%)
  local copies, waits for them, and re-layouts  7.22 us (3%)
    pallas_call x1, Pallas kernels, shards(): pl.pallas_call(functools.partial(main_kernel, n_spec, n_wave), out_shape=...  268 us
    unnamed x14, local copies, waits for them, and re-layouts  6.44 us

profile of v4, /device:TPU:24, one launch (start us, length us, event | category | flops | bytes accessed | tf_op | source)
XLA Modules:
  0.0 280.7 jit_solution(12136966618825612457)
XLA Ops:
  0.6 0.0 copy-start
  0.7 0.8 and_select_fusion
  1.4 0.1 broadcast_bitcast_fusion
  1.5 0.7 broadcast_bitcast_fusion.1
  2.2 0.7 fusion.1
  2.9 0.0 copy-done
  2.9 0.2 broadcast_in_dim.16.lo_ref
  3.1 0.2 broadcast_in_dim.14.lo_ref
  3.3 0.2 broadcast_in_dim.15.hi_ref
  3.5 0.2 broadcast_in_dim.17.hi_ref
  3.7 0.0 copy-start.2
  3.8 2.0 copy-done.2
  5.8 0.0 copy-start.3
  5.8 3.3 %shard_map.77.rest_ref = bf16[1024,1920]{1,0:T(8,128)(2,1)S(1)} custom-call(s32[4]{0:T(128)S(1)} %get-tuple-element.3.shift_ref, bf16[1024,1792]{1,0:T(8,128)(2,1)S(1)} %copy-done.2, s32[1024,128]{1,0:T(8,128)S(1)} %broadcast_in_dim.14.lo_ref, s32[1024,128]{1,0:T(8,128)S(1)} %broadcast_in_dim.15.hi_ref), custom_call_target="tpu_custom_call" | custom-call | tf_op jit(solution)/shard_map/pallas_call | solution.py:38
  9.1 0.0 copy-start.1
  9.2 1.9 copy-done.1
  11.0 0.0 copy-done.3
  11.0 267.9 %shard_map.78 = (f32[128,1792]{1,0:T(8,128)S(1)}, f32[1024,128]{1,0:T(8,128)S(1)}) custom-call(s32[4]{0:T(128)S(1)} %get-tuple-element.2.first_ref, bf16[1024,1920]{1,0:T(8,128)(2,1)} %copy-done.1, s32[1024,128]{1,0:T(8,128)S(1)} %broadcast_in_dim.16.lo_ref, s32[1024,128]{1,0:T(8,128)S(1)} %broadcast_in_dim.17.hi_ref, f32[1024,128]{1,0:T(8,128)S(1)} %copy-done.3, ...), custom_call_target="tpu_custom_call" | custom-call | tf_op jit(solution)/shard_map/pallas_call | solution.py:513
  279.0 0.9 copy.15
  279.9 0.8 copy.16
  (3 shorter events, 0.0 us)
Async XLA Ops:
  0.6 2.3 copy-start
  3.7 2.0 copy-start.2
  5.8 5.2 %copy-start.3 = (f32[1024,128]{1,0:T(8,128)S(1)}, f32[1024,128]{1,0:T(8,128)}, u32[]{:S(2)}) copy-start(f32[1024,128]{1,0:T(8,128)} %coef_ref.1) | copy-start | bytes 1572868
  9.1 1.9 copy-start.1
